TPU v7x, 32 devices: a whole 2x2x4 slice. The times are simulated.
32 devices in a mesh: slab: 8 (over y, x, core), field: 4 (over z).
Axes of the slice: x: 2, y: 2, z: 4, core: 2. Of those that a mesh axis runs over, the one named last changes fastest.
Arguments:
- snaps: bfloat16 [4, 16, 3, 32, 2048], P('field', 'slab'), may hold values from -6 to 6
- writer_map: int32 [64], replicated, may hold values from 0 to 63, each once
- omega: int32 [64, 64], replicated, may hold values from -3 to 3
- face_level: int32 [32], replicated, may hold values from 0 to 11
Outputs:
- sketch_rows: float32 [4, 16, 64], P('field')
- core: float32 [64, 64], replicated
All inputs are finite; a program needn't handle non-finite values.
Results may differ from a plain program's by a relative error of at most 0.00035.
Values may be sent and summed in bfloat16 or wider, within the bound.
A program may use at most 128 MiB of HBM per device.

v0:
```python
import jax
import jax.numpy as jnp
from jax import lax
from jax.sharding import PartitionSpec as P


def from_behind(block, axis, distance):
    devices = range(lax.axis_size(axis))
    route = [(i - distance, i) for i in devices if i - distance in devices]
    return lax.ppermute(block, axis, route)


def body(snaps, writer_map, omega, face_level):
    field_count = lax.axis_size("field")
    slab_at = lax.axis_index("slab")
    field_at = lax.axis_index("field")
    sketch_cols = omega.shape[1]
    total_snaps = omega.shape[0]
    total_planes = face_level.shape[0]
    group_rows = total_snaps // field_count
    columns = jnp.arange(total_snaps, dtype=jnp.int32)
    onehot = (writer_map[:, None] == columns[None, :]).astype(jnp.bfloat16)
    test_all = jnp.dot(
        onehot, omega.astype(jnp.bfloat16), preferred_element_type=jnp.float32
    ).astype(jnp.bfloat16)
    local = lax.all_to_all(snaps, "slab", split_axis=3, concat_axis=1, tiled=True)
    comps = local.shape[2]
    planes_dev = local.shape[3]
    cells = local.shape[4]
    features = comps * planes_dev * cells
    test_own = lax.dynamic_slice_in_dim(test_all, field_at * group_rows, group_rows, 0)
    flat = local.reshape(group_rows, features)
    partial_z = jnp.dot(test_own.T, flat, preferred_element_type=jnp.float32)
    sketched = lax.psum(partial_z.astype(jnp.bfloat16), "field").astype(jnp.float32)
    sketched = sketched.reshape(sketch_cols, comps, planes_dev, cells)
    spacing = 0.5 * jnp.power(jnp.float32(1.12), face_level.astype(jnp.float32))
    first_plane = slab_at * planes_dev
    weight = lax.dynamic_slice_in_dim(spacing, first_plane, planes_dev, 0).reshape(
        1, 1, planes_dev, 1
    )
    coupling = lax.dynamic_slice_in_dim(1.0 / spacing, first_plane, planes_dev, 0).reshape(
        1, 1, planes_dev, 1
    )
    scale = 1.0 / (comps * total_planes * cells)
    lower = from_behind(
        sketched[:, :, -1:].astype(jnp.bfloat16), ("slab", "field"), field_count
    ).astype(jnp.float32)
    below = jnp.concatenate([lower, sketched[:, :, :-1]], axis=2)
    flux = coupling * (sketched - below)
    upper = from_behind(
        flux[:, :, :1].astype(jnp.bfloat16), ("slab", "field"), -field_count
    ).astype(jnp.float32)
    above = jnp.concatenate([flux[:, :, 1:], upper], axis=2)
    applied = (
        ((weight * sketched + flux - above) * scale)
        .astype(jnp.bfloat16)
        .reshape(sketch_cols, features)
    )
    partial_rows = lax.dot_general(
        flat, applied, (((1,), (1,)), ((), ())), preferred_element_type=jnp.float32
    )
    blocks = (jnp.arange(field_count, dtype=jnp.int32) == field_at).astype(jnp.float32)
    stored_rows = (blocks[:, None, None] * partial_rows[None, :, :]).reshape(
        total_snaps, sketch_cols
    )
    rows = lax.psum(stored_rows, ("slab", "field"))
    core = (
        jnp.dot(test_all.astype(jnp.float32).T, rows, precision=lax.Precision.HIGHEST) / total_snaps
    )
    own_rows = lax.dynamic_slice_in_dim(rows, field_at * group_rows, group_rows, 0)
    return (own_rows.reshape(1, group_rows, sketch_cols), core)


def solution(mesh):
    in_specs = (P("field", "slab", None, None, None), P(), P(), P())
    out_specs = (P("field", None, None), P())
    return jax.shard_map(body, mesh=mesh, in_specs=in_specs, out_specs=out_specs, check_vma=False)
```

profile of v0, /device:TPU:0, one launch (start us, length us, event | category | flops | bytes accessed | tf_op | source)
XLA Modules:
  0.0 285.8 jit_solution(11686878091657337957)
XLA Ops:
  7.2 2.8 copy.7
  10.0 5.2 %all-to-all-start = ((bf16[1,2,3,32,2048]{4,2,1,0,3:T(4,128)(2,1)}), bf16[1,2,3,32,2048]{4,2,1,0,3:T(4,128)(2,1)S(1)}, u32[]{:S(2)}, u32[]{:S(2)}) async-start(bf16[1,2,3,32,2048]{4,2,1,0,3:T(4,128)(2,1)} %copy.7), calls=%async_computation | async-start | bytes 2097152 | tf_op jit(solution)/shard_map/all_to_all | solution.py:26
  15.2 1.0 convolution_convert_fusion.1
  16.2 14.4 %all-to-all-done = bf16[1,2,3,32,2048]{4,2,1,0,3:T(4,128)(2,1)S(1)} async-done(((bf16[1,2,3,32,2048]{4,2,1,0,3:T(4,128)(2,1)}), bf16[1,2,3,32,2048]{4,2,1,0,3:T(4,128)(2,1)S(1)}, u32[]{:S(2)}, u32[]{:S(2)}) %all-to-all-start) | async-done | bytes 786464 | tf_op jit(solution)/shard_map/all_to_all | solution.py:26
  30.5 0.9 copy.18
  31.5 0.6 reshape.33
  32.1 2.7 convolution_convert_fusion
  34.8 120.6 %all-reduce.2.cloned.1.call-done = bf16[64,24576]{1,0:T(8,128)(2,1)} async-done(((bf16[64,24576]{1,0:T(8,128)(2,1)}), bf16[64,24576]{1,0:T(8,128)(2,1)}) %all-reduce.2.cloned.1.call-update) | async-done | bytes 3145744 | tf_op jit(solution)/shard_map/psum | solution.py:34
  155.4 7.9 %reshape.34 = f32[64,3,4,2048]{3,2,1,0:T(4,128)} reshape(bf16[64,24576]{1,0:T(8,128)(2,1)} %all-reduce.2.cloned.1.call-done) | data formatting | bytes 9437184 | tf_op jit(solution)/shard_map/reshape | solution.py:35
  163.3 4.5 %slice.25 = bf16[64,3,1,2048]{3,2,1,0:T(2,128)(2,1)S(1)} slice(f32[64,3,4,2048]{3,2,1,0:T(4,128)} %reshape.34), slice={[0:64], [0:3], [3:4], [0:2048]} | slice | bytes 1572864 | tf_op jit(solution)/shard_map/slice | solution.py:46
  167.8 0.5 copy.20
  168.2 1.9 collective-permute-start
  170.3 2.3 slice-done.2
  172.6 2.7 copy.19
  175.4 0.2 convert_element_type.42
  175.6 5.9 %pad_maximum_fusion = (f32[64,3,4,2048]{3,0,2,1:T(8,128)}, f32[64,3,4,2048]{3,0,2,1:T(8,128)S(1)}) fusion(f32[64,3,3,2048]{3,0,2,1:T(8,128)S(1)} %copy.19, f32[64,3,1,2048]{3,0,2,1:T(8,128)S(1)} %convert_element_type.42, f32[64,3,4,2048]{3,2,1,0:T(4,128)S(1)} %bitcast.21, f32[4]{0:T(128)S(1)} %dynamic_slice.14), kind=kLoop, calls=%fused_computation.1 | loop fusion | flops 4718592 | bytes 25165840 | tf_op jit(solution)/shard_map/concatenate | solution.py:48
  181.5 2.8 copy-done
  184.3 0.1 slice.24
  184.4 1.3 collective-permute-start.1
  185.9 0.1 broadcast_bitcast_fusion.1
  186.1 0.1 mul.71
  186.2 5.1 %slice.20 = f32[64,3,3,2048]{3,0,2,1:T(8,128)} slice(f32[64,3,4,2048]{3,0,2,1:T(8,128)} %copy-done), slice={[0:64], [0:3], [1:4], [0:2048]} | slice | bytes 9437184 | tf_op jit(solution)/shard_map/slice | solution.py:53
  191.3 6.7 %copy.11 = f32[64,3,4,2048]{3,2,1,0:T(4,128)} copy(f32[64,3,4,2048]{3,0,2,1:T(8,128)S(1)} %bitcast.23) | data formatting | bytes 12582912 | tf_op jit(solution)/shard_map/concatenate | solution.py:48
  198.0 8.0 %concatenate.11 = f32[64,24576]{1,0:T(8,128)} reshape(f32[64,3,4,2048]{3,2,1,0:T(4,128)} %copy.11) | data formatting | bytes 12582912 | tf_op jit(solution)/shard_map/concatenate | solution.py:48
  206.0 1.3 convert_element_type.43
  207.3 2.8 pad_maximum_fusion.1
  210.1 6.6 %copy.13 = f32[64,3,4,2048]{3,2,1,0:T(4,128)} copy(f32[64,3,4,2048]{3,0,2,1:T(8,128)S(1)} %pad_maximum_fusion.1) | data formatting | bytes 12582912 | tf_op jit(solution)/shard_map/concatenate | solution.py:53
  216.7 8.1 %concatenate.13 = f32[64,24576]{1,0:T(8,128)} reshape(f32[64,3,4,2048]{3,2,1,0:T(4,128)} %copy.13) | data formatting | bytes 12582912 | tf_op jit(solution)/shard_map/concatenate | solution.py:53
  224.8 6.4 %fusion.2 = f32[16,64]{1,0:T(8,128)S(1)} fusion(bf16[16,24576]{1,0:T(8,128)(2,1)} %copy-done.2, f32[64,24576]{1,0:T(8,128)} %concatenate.13, f32[64,24576]{1,0:T(8,128)} %concatenate.11, f32[24576]{0:T(1024)S(1)} %bitcast.26, f32[24576]{0:T(1024)S(1)} %bitcast.27, bf16[64,24576]{1,0:T(8,128)(2,1)S(1)} %copy-done.1), kind=kOutput, calls=%fused_computation.11 | convolution fusion | flops 62914560 | bytes 16715776 | tf_op jit(solution)/shard_map/dot_general | solution.py:59
  231.3 46.2 %psum.15 = f32[64,64]{1,0:T(8,128)S(1)} all-reduce(f32[64,64]{1,0:T(8,128)S(1)} %bitcast_multiply_fusion), channel_id=1, replica_groups=mesh['slab'=8,'field'=4] {'slab','field'}, use_global_device_ids=true, to_apply=%region_1.0 | all-reduce | flops 4096 | bytes 32768 | tf_op jit(solution)/shard_map/psum | solution.py:66
  277.5 0.8 convolution_multiply_fusion
  278.3 0.6 dynamic-slice_bitcast_fusion
  (31 shorter events, 0.5 us)
Async XLA Ops:
  10.0 20.6 %all-to-all-start = ((bf16[1,2,3,32,2048]{4,2,1,0,3:T(4,128)(2,1)}), bf16[1,2,3,32,2048]{4,2,1,0,3:T(4,128)(2,1)S(1)}, u32[]{:S(2)}, u32[]{:S(2)}) async-start(bf16[1,2,3,32,2048]{4,2,1,0,3:T(4,128)(2,1)} %copy.7), calls=%async_computation | async-start | bytes 2097152 | tf_op jit(solution)/shard_map/all_to_all | solution.py:26
  15.1 140.3 %all-reduce.2.cloned.1.call-start = ((), (), s32[]{:S(2)}) async-start(), calls=%async_computation.1 | async-start | bytes 6291456 | tf_op jit(solution)/shard_map/psum | solution.py:34
  32.1 131.2 %copy-start.2 = (bf16[16,24576]{1,0:T(8,128)(2,1)}, bf16[16,24576]{1,0:T(8,128)(2,1)S(1)}, u32[]{:S(2)}) copy-start(bf16[16,24576]{1,0:T(8,128)(2,1)S(1)} %reshape.33) | copy-start | bytes 2359300
  34.8 135.4 %copy-start.3 = (s32[32]{0:T(128)S(1)}, s32[32]{0:T(128)}, u32[]{:S(2)}) copy-start(s32[32]{0:T(128)} %param.7) | copy-start | bytes 388
  168.2 7.1 %collective-permute-start = (bf16[64,3,1,2048]{3,0,2,1:T(8,128)(2,1)S(1)}, bf16[64,3,1,2048]{3,0,2,1:T(8,128)(2,1)S(1)}, u32[]{:S(2)}, u32[]{:S(2)}) collective-permute-start(bf16[64,3,1,2048]{3,0,2,1:T(8,128)(2,1)S(1)} %copy.20), channel_id=1, source_target_pairs={{0,4},{1,5},{2,6},{3,7},{4,8},{5,9},{6,10},{7,11},{8,12},{9,13},{1... | collective-permute-start | bytes 2359304 | tf_op jit(solution)/shard_map/ppermute | solution.py:10
  170.3 2.3 slice-start.2
  170.3 5.3 %slice-start = ((s8[6291456]{0:T(1024)(128)(4,1)}), s8[4194304]{0:T(1024)(128)(4,1)S(1)}, s32[]{:S(2)}) async-start(s8[6291456]{0:T(1024)(128)(4,1)} %bitcast.20), calls=%async_computation.2 | async-start | bytes 8388608
  172.6 2.9 %slice-start.1 = ((s8[6291456]{0:T(1024)(128)(4,1)}), s8[2097152]{0:T(1024)(128)(4,1)S(1)}, s32[]{:S(2)}) async-start(s8[6291456]{0:T(1024)(128)(4,1)} %bitcast.20), calls=%async_computation.3 | async-start | bytes 4194304
  181.5 2.8 copy-start
  181.5 9.9 %slice-start.3 = ((s8[6291456]{0:T(1024)(128)(4,1)}), s8[2097152]{0:T(1024)(128)(4,1)S(1)}, s32[]{:S(2)}) async-start(s8[6291456]{0:T(1024)(128)(4,1)} %bitcast.22), calls=%async_computation.5 | async-start | bytes 4194304
  184.4 21.6 %collective-permute-start.1 = (bf16[64,3,1,2048]{3,0,2,1:T(8,128)(2,1)S(1)}, bf16[64,3,1,2048]{3,0,2,1:T(8,128)(2,1)}, u32[]{:S(2)}, u32[]{:S(2)}) collective-permute-start(bf16[64,3,1,2048]{3,0,2,1:T(8,128)(2,1)S(1)} %slice.24), channel_id=1, source_target_pairs={{4,0},{5,1},{6,2},{7,3},{8,4},{9,5},{10,6},{11,7},{12,8},{13,9},{1... | collective-permute-start | bytes 2359304 | tf_op jit(solution)/shard_map/ppermute | solution.py:10
  186.2 5.1 %slice-start.4 = ((s8[6291456]{0:T(1024)(128)(4,1)}), s8[4194304]{0:T(1024)(128)(4,1)S(1)}, s32[]{:S(2)}) async-start(s8[6291456]{0:T(1024)(128)(4,1)} %bitcast.22), calls=%async_computation.6 | async-start | bytes 8388608
  216.7 8.1 %copy-start.1 = (bf16[64,24576]{1,0:T(8,128)(2,1)S(1)}, bf16[64,24576]{1,0:T(8,128)(2,1)}, u32[]{:S(2)}) copy-start(bf16[64,24576]{1,0:T(8,128)(2,1)} %all-reduce.2.cloned.1.call-done) | copy-start | bytes 9437188
Sparse Core Ops, SparseCore 0:
  34.9 120.4 all-reduce.1
where the time goes:
time: 286 us
  waiting for transfers between devices  135 us (47%)
  local copies, waits for them, and re-layouts  60.8 us (21%)
  blocking collectives  46.2 us (16%)
  between operations  14.2 us (5%)
  matrix products  10.9 us (4%)
  other arithmetic  10.2 us (4%)
  starting transfers between devices  8.43 us (3%)
    psum x1, waiting for transfers between devices, body(): lax.psum(partial_z.astype(jnp.bfloat16), 'field').astype(jnp.float32)  121 us
    psum x1, blocking collectives, body(): rows = lax.psum(stored_rows, ('slab', 'field'))  46.2 us
    concatenate x2, local copies, waits for them, and re-layouts, body(): above = jnp.concatenate([flux[:, :, 1:], upper], axis=2)  14.7 us
    concatenate x2, local copies, waits for them, and re-layouts, body(): below = jnp.concatenate([lower, sketched[:, :, :-1]], axis=2)  14.6 us
    all_to_all x1, waiting for transfers between devices, body(): lax.all_to_all(snaps, 'slab', split_axis=3, concat_axis=1, tiled=True)  14.4 us
    unnamed x23, local copies, waits for them, and re-layouts  9.04 us
    reshape x1, local copies, waits for them, and re-layouts, body(): sketched = sketched.reshape(sketch_cols, comps, planes_dev, cells)  7.87 us
    dot_general x1, matrix products, body(): lax.dot_general(flat, applied, (((1,), (1,)), ((), ())), preferred_elemen...  6.4 us
  transfers between devices with their start and end apart: 4, of which 2 were waited for; matrix products, arithmetic and copies ran while one was open for 8% of the time, Pallas kernels for 0%

commit v1 on v0

--- a/solution.py
+++ b/solution.py
@@ -63,7 +63,7 @@
     stored_rows = (blocks[:, None, None] * partial_rows[None, :, :]).reshape(
         total_snaps, sketch_cols
     )
-    rows = lax.psum(stored_rows, ("slab", "field"))
+    rows = lax.psum(lax.psum(stored_rows, "slab"), "field")
     core = (
         jnp.dot(test_all.astype(jnp.float32).T, rows, precision=lax.Precision.HIGHEST) / total_snaps
     )

time: 286 us -> 290 us (1.014)
  blocking collectives: 46.2 us -> 49.3 us
    psum x1 -> x2, blocking collectives: 46.2 us -> 49.3 us  [body(): rows = lax.psum(lax.psum(stored_rows, 'slab'), 'field')]
where the time goes in v1:
time: 290 us; the launch traced here: 289 us
  waiting for transfers between devices  135 us (47%)
  local copies, waits for them, and re-layouts  60.8 us (21%)
  blocking collectives  49.3 us (17%)
  between operations  14.2 us (5%)
  matrix products  10.8 us (4%)
  other arithmetic  10.3 us (4%)
  starting transfers between devices  8.43 us (3%)
    psum x1, waiting for transfers between devices, body(): lax.psum(partial_z.astype(jnp.bfloat16), 'field').astype(jnp.float32)  121 us
    psum x2, blocking collectives, body(): rows = lax.psum(lax.psum(stored_rows, 'slab'), 'field')  49.3 us
    concatenate x2, local copies, waits for them, and re-layouts, body(): above = jnp.concatenate([flux[:, :, 1:], upper], axis=2)  14.7 us
    concatenate x2, local copies, waits for them, and re-layouts, body(): below = jnp.concatenate([lower, sketched[:, :, :-1]], axis=2)  14.6 us
    all_to_all x1, waiting for transfers between devices, body(): lax.all_to_all(snaps, 'slab', split_axis=3, concat_axis=1, tiled=True)  14.4 us
    unnamed x23, local copies, waits for them, and re-layouts  9.03 us
    reshape x1, local copies, waits for them, and re-layouts, body(): sketched = sketched.reshape(sketch_cols, comps, planes_dev, cells)  7.86 us
    dot_general x1, matrix products, body(): lax.dot_general(flat, applied, (((1,), (1,)), ((), ())), preferred_elemen...  6.4 us
  transfers between devices with their start and end apart: 4, of which 2 were waited for; matrix products, arithmetic and copies ran while one was open for 8% of the time, Pallas kernels for 0%

profile of v1, /device:TPU:0, one launch (start us, length us, event | category | flops | bytes accessed | tf_op | source)
XLA Modules:
  0.0 288.8 jit_solution(5655374758496263184)
XLA Ops:
  7.2 2.8 copy.7
  10.0 5.2 %all-to-all-start = ((bf16[1,2,3,32,2048]{4,2,1,0,3:T(4,128)(2,1)}), bf16[1,2,3,32,2048]{4,2,1,0,3:T(4,128)(2,1)S(1)}, u32[]{:S(2)}, u32[]{:S(2)}) async-start(bf16[1,2,3,32,2048]{4,2,1,0,3:T(4,128)(2,1)} %copy.7), calls=%async_computation | async-start | bytes 2097152 | tf_op jit(solution)/shard_map/all_to_all | solution.py:26
  15.2 1.0 convolution_convert_fusion.1
  16.1 14.4 %all-to-all-done = bf16[1,2,3,32,2048]{4,2,1,0,3:T(4,128)(2,1)S(1)} async-done(((bf16[1,2,3,32,2048]{4,2,1,0,3:T(4,128)(2,1)}), bf16[1,2,3,32,2048]{4,2,1,0,3:T(4,128)(2,1)S(1)}, u32[]{:S(2)}, u32[]{:S(2)}) %all-to-all-start) | async-done | bytes 786464 | tf_op jit(solution)/shard_map/all_to_all | solution.py:26
  30.5 0.9 copy.18
  31.5 0.6 reshape.33
  32.1 2.6 convolution_convert_fusion
  34.7 120.6 %all-reduce.2.cloned.1.call-done = bf16[64,24576]{1,0:T(8,128)(2,1)} async-done(((bf16[64,24576]{1,0:T(8,128)(2,1)}), bf16[64,24576]{1,0:T(8,128)(2,1)}) %all-reduce.2.cloned.1.call-update) | async-done | bytes 3145744 | tf_op jit(solution)/shard_map/psum | solution.py:34
  155.4 7.9 %reshape.34 = f32[64,3,4,2048]{3,2,1,0:T(4,128)} reshape(bf16[64,24576]{1,0:T(8,128)(2,1)} %all-reduce.2.cloned.1.call-done) | data formatting | bytes 9437184 | tf_op jit(solution)/shard_map/reshape | solution.py:35
  163.2 4.5 %slice.25 = bf16[64,3,1,2048]{3,2,1,0:T(2,128)(2,1)S(1)} slice(f32[64,3,4,2048]{3,2,1,0:T(4,128)} %reshape.34), slice={[0:64], [0:3], [3:4], [0:2048]} | slice | bytes 1572864 | tf_op jit(solution)/shard_map/slice | solution.py:46
  167.7 0.5 copy.20
  168.2 1.9 collective-permute-start
  170.2 2.3 slice-done.2
  172.6 2.7 copy.19
  175.3 0.2 convert_element_type.42
  175.5 5.9 %pad_maximum_fusion = (f32[64,3,4,2048]{3,0,2,1:T(8,128)}, f32[64,3,4,2048]{3,0,2,1:T(8,128)S(1)}) fusion(f32[64,3,3,2048]{3,0,2,1:T(8,128)S(1)} %copy.19, f32[64,3,1,2048]{3,0,2,1:T(8,128)S(1)} %convert_element_type.42, f32[64,3,4,2048]{3,2,1,0:T(4,128)S(1)} %bitcast.21, f32[4]{0:T(128)S(1)} %dynamic_slice.14), kind=kLoop, calls=%fused_computation.1 | loop fusion | flops 4718592 | bytes 25165840 | tf_op jit(solution)/shard_map/concatenate | solution.py:48
  181.5 2.8 copy-done
  184.3 0.1 slice.24
  184.4 1.3 collective-permute-start.1
  186.1 0.1 mul.71
  186.2 5.1 %slice.20 = f32[64,3,3,2048]{3,0,2,1:T(8,128)} slice(f32[64,3,4,2048]{3,0,2,1:T(8,128)} %copy-done), slice={[0:64], [0:3], [1:4], [0:2048]} | slice | bytes 9437184 | tf_op jit(solution)/shard_map/slice | solution.py:53
  191.3 6.7 %copy.11 = f32[64,3,4,2048]{3,2,1,0:T(4,128)} copy(f32[64,3,4,2048]{3,0,2,1:T(8,128)S(1)} %bitcast.23) | data formatting | bytes 12582912 | tf_op jit(solution)/shard_map/concatenate | solution.py:48
  198.0 8.0 %concatenate.11 = f32[64,24576]{1,0:T(8,128)} reshape(f32[64,3,4,2048]{3,2,1,0:T(4,128)} %copy.11) | data formatting | bytes 12582912 | tf_op jit(solution)/shard_map/concatenate | solution.py:48
  206.0 1.3 convert_element_type.43
  207.3 2.8 pad_maximum_fusion.1
  210.1 6.6 %copy.13 = f32[64,3,4,2048]{3,2,1,0:T(4,128)} copy(f32[64,3,4,2048]{3,0,2,1:T(8,128)S(1)} %pad_maximum_fusion.1) | data formatting | bytes 12582912 | tf_op jit(solution)/shard_map/concatenate | solution.py:53
  216.7 8.1 %concatenate.13 = f32[64,24576]{1,0:T(8,128)} reshape(f32[64,3,4,2048]{3,2,1,0:T(4,128)} %copy.13) | data formatting | bytes 12582912 | tf_op jit(solution)/shard_map/concatenate | solution.py:53
  224.8 6.4 %fusion.2 = f32[16,64]{1,0:T(8,128)S(1)} fusion(bf16[16,24576]{1,0:T(8,128)(2,1)} %copy-done.2, f32[64,24576]{1,0:T(8,128)} %concatenate.13, f32[64,24576]{1,0:T(8,128)} %concatenate.11, f32[24576]{0:T(1024)S(1)} %bitcast.26, f32[24576]{0:T(1024)S(1)} %bitcast.27, bf16[64,24576]{1,0:T(8,128)(2,1)S(1)} %copy-done.1), kind=kOutput, calls=%fused_computation.11 | convolution fusion | flops 62914560 | bytes 16715776 | tf_op jit(solution)/shard_map/dot_general | solution.py:59
  231.3 32.4 %psum.22 = f32[64,64]{1,0:T(8,128)S(1)} all-reduce(f32[64,64]{1,0:T(8,128)S(1)} %bitcast_multiply_fusion), channel_id=1, replica_groups=mesh['slab'=8,'field'=4] {'slab'}, use_global_device_ids=true, to_apply=%region_1.0 | all-reduce | flops 4096 | bytes 32768 | tf_op jit(solution)/shard_map/psum | solution.py:66
  263.6 16.9 %psum.23 = f32[64,64]{1,0:T(8,128)S(1)} all-reduce(f32[64,64]{1,0:T(8,128)S(1)} %psum.22), channel_id=1, replica_groups=mesh['slab'=8,'field'=4] {'field'}, use_global_device_ids=true, to_apply=%region_2.0 | all-reduce | flops 4096 | bytes 32768 | tf_op jit(solution)/shard_map/psum | solution.py:66
  280.6 0.8 convolution_multiply_fusion
  281.4 0.6 dynamic-slice_bitcast_fusion
  (32 shorter events, 0.6 us)
Async XLA Ops:
  10.0 20.6 %all-to-all-start = ((bf16[1,2,3,32,2048]{4,2,1,0,3:T(4,128)(2,1)}), bf16[1,2,3,32,2048]{4,2,1,0,3:T(4,128)(2,1)S(1)}, u32[]{:S(2)}, u32[]{:S(2)}) async-start(bf16[1,2,3,32,2048]{4,2,1,0,3:T(4,128)(2,1)} %copy.7), calls=%async_computation | async-start | bytes 2097152 | tf_op jit(solution)/shard_map/all_to_all | solution.py:26
  15.1 140.2 %all-reduce.2.cloned.1.call-start = ((), (), s32[]{:S(2)}) async-start(), calls=%async_computation.1 | async-start | bytes 6291456 | tf_op jit(solution)/shard_map/psum | solution.py:34
  32.1 131.2 %copy-start.2 = (bf16[16,24576]{1,0:T(8,128)(2,1)}, bf16[16,24576]{1,0:T(8,128)(2,1)S(1)}, u32[]{:S(2)}) copy-start(bf16[16,24576]{1,0:T(8,128)(2,1)S(1)} %reshape.33) | copy-start | bytes 2359300
  34.7 135.4 %copy-start.3 = (s32[32]{0:T(128)S(1)}, s32[32]{0:T(128)}, u32[]{:S(2)}) copy-start(s32[32]{0:T(128)} %param.7) | copy-start | bytes 388
  168.2 7.1 %collective-permute-start = (bf16[64,3,1,2048]{3,0,2,1:T(8,128)(2,1)S(1)}, bf16[64,3,1,2048]{3,0,2,1:T(8,128)(2,1)S(1)}, u32[]{:S(2)}, u32[]{:S(2)}) collective-permute-start(bf16[64,3,1,2048]{3,0,2,1:T(8,128)(2,1)S(1)} %copy.20), channel_id=1, source_target_pairs={{0,4},{1,5},{2,6},{3,7},{4,8},{5,9},{6,10},{7,11},{8,12},{9,13},{1... | collective-permute-start | bytes 2359304 | tf_op jit(solution)/shard_map/ppermute | solution.py:10
  170.2 2.3 slice-start.2
  170.2 5.3 %slice-start = ((s8[6291456]{0:T(1024)(128)(4,1)}), s8[4194304]{0:T(1024)(128)(4,1)S(1)}, s32[]{:S(2)}) async-start(s8[6291456]{0:T(1024)(128)(4,1)} %bitcast.20), calls=%async_computation.2 | async-start | bytes 8388608
  172.6 2.9 %slice-start.1 = ((s8[6291456]{0:T(1024)(128)(4,1)}), s8[2097152]{0:T(1024)(128)(4,1)S(1)}, s32[]{:S(2)}) async-start(s8[6291456]{0:T(1024)(128)(4,1)} %bitcast.20), calls=%async_computation.3 | async-start | bytes 4194304
  181.5 2.8 copy-start
  181.5 9.9 %slice-start.3 = ((s8[6291456]{0:T(1024)(128)(4,1)}), s8[2097152]{0:T(1024)(128)(4,1)S(1)}, s32[]{:S(2)}) async-start(s8[6291456]{0:T(1024)(128)(4,1)} %bitcast.22), calls=%async_computation.5 | async-start | bytes 4194304
  184.4 21.6 %collective-permute-start.1 = (bf16[64,3,1,2048]{3,0,2,1:T(8,128)(2,1)S(1)}, bf16[64,3,1,2048]{3,0,2,1:T(8,128)(2,1)}, u32[]{:S(2)}, u32[]{:S(2)}) collective-permute-start(bf16[64,3,1,2048]{3,0,2,1:T(8,128)(2,1)S(1)} %slice.24), channel_id=1, source_target_pairs={{4,0},{5,1},{6,2},{7,3},{8,4},{9,5},{10,6},{11,7},{12,8},{13,9},{1... | collective-permute-start | bytes 2359304 | tf_op jit(solution)/shard_map/ppermute | solution.py:10
  186.2 5.2 %slice-start.4 = ((s8[6291456]{0:T(1024)(128)(4,1)}), s8[4194304]{0:T(1024)(128)(4,1)S(1)}, s32[]{:S(2)}) async-start(s8[6291456]{0:T(1024)(128)(4,1)} %bitcast.22), calls=%async_computation.6 | async-start | bytes 8388608
  216.7 8.1 %copy-start.1 = (bf16[64,24576]{1,0:T(8,128)(2,1)S(1)}, bf16[64,24576]{1,0:T(8,128)(2,1)}, u32[]{:S(2)}) copy-start(bf16[64,24576]{1,0:T(8,128)(2,1)} %all-reduce.2.cloned.1.call-done) | copy-start | bytes 9437188
Sparse Core Ops, SparseCore 0:
  34.9 120.4 all-reduce.1
